TPU v7x, 32 devices: a whole 2x2x4 slice. The times are simulated.
32 devices in a mesh: ctx: 4 (over z), exp: 8 (over y, x, core).
Axes of the slice: x: 2, y: 2, z: 4, core: 2. Of those that a mesh axis runs over, the one named last changes fastest.
Arguments:
- queries: bfloat16 [8, 256, 1024], P('exp', 'ctx'), may hold values from -6 to 6
- keys: bfloat16 [8, 256, 1024], P('exp', 'ctx'), may hold values from -6 to 6
- values: bfloat16 [8, 256, 1024], P('exp', 'ctx'), may hold values from -6 to 6
- residual: bfloat16 [8, 256, 2048], P('exp', 'ctx'), may hold values from -6 to 6
- out_proj: bfloat16 [1024, 2048], replicated, may hold values from -0.1875 to 0.1875
- norm_gain: float32 [2048], replicated, may hold values from 0.25 to 1.75
- w_gate: bfloat16 [8, 2048, 512], P('exp'), may hold values from -0.125 to 0.125
- w_up: bfloat16 [8, 2048, 512], P('exp'), may hold values from -0.125 to 0.125
- w_down: bfloat16 [8, 512, 2048], P('exp'), may hold values from -0.25 to 0.25
- routes: int32 [8, 256, 4], P('exp', 'ctx'), may hold values from 0 to 7, all different within a row; in each aligned block of 64 rows (0 to 63, 64 to 127, ..., all dimensions but the last counted through in order) at most 48 rows name the same one
- route_prob: float32 [8, 256, 4], P('exp', 'ctx'), may hold values from 0.05 to 0.8
Outputs:
- mixed: bfloat16 [8, 256, 2048], P('exp', 'ctx')
Inputs may be any that keep to these rules, and one draw needn't show every extreme that they name: `routes`: each row names 4 different experts; the 64 rows of one device name no expert more than 48 times, and in some devices' rows one expert exactly 48 times.
All inputs are finite; a program needn't handle non-finite values.
Results may differ from a plain program's by a relative error of at most 0.008.
Values may be sent and summed in bfloat16 or wider, within the bound.
A program may use at most 64 MiB of HBM per device.

v0:
```python
import jax
import jax.numpy as jnp
from jax import lax
from jax.sharding import PartitionSpec as P

HEADS = 8
HEAD_DIM = 128
TOP = 4


neg_big = -1e30


def passed_along(block, axis, distance):
    devices = range(lax.axis_size(axis))
    route = [(i - distance, i) for i in devices if i - distance in devices]
    return lax.ppermute(block, axis, route)


def attend_piece(softmax_state, query_heads, query_pos, key_piece, piece_start):
    run_max, run_sum, run_acc = softmax_state
    length = key_piece.shape[1]
    key_rows = key_piece[0].reshape(length, HEADS, HEAD_DIM)
    value_rows = key_piece[1].reshape(length, HEADS, HEAD_DIM)
    scale = HEAD_DIM ** (-0.5)
    scores = jnp.einsum("hqd,khd->hqk", query_heads, key_rows, preferred_element_type=jnp.float32)
    key_pos = piece_start + jnp.arange(length, dtype=jnp.int32)
    allowed = key_pos[None, :] <= query_pos[:, None]
    scores = jnp.where(allowed[None], scores, neg_big)
    new_max = jnp.maximum(run_max, scores.max(axis=-1))
    rescale = jnp.exp((run_max - new_max) * scale)
    exponent = jnp.where(allowed[None], jnp.exp((scores - new_max[:, :, None]) * scale), 0.0)
    run_sum = run_sum * rescale + exponent.sum(axis=-1)
    update = jnp.einsum(
        "hqk,khd->hqd",
        exponent.astype(jnp.bfloat16),
        value_rows,
        preferred_element_type=jnp.float32,
    )
    run_acc = run_acc * rescale[:, :, None] + update
    return (new_max, run_sum, run_acc)


def local(
    queries, keys, values, residual, out_proj, norm_gain, w_gate, w_up, w_down, routes, route_prob
):
    tok_count = queries.shape[1]
    my_index = lax.axis_index("ctx")
    query_pos = my_index * tok_count + jnp.arange(tok_count, dtype=jnp.int32)
    query_heads = jnp.transpose(queries[0].reshape(tok_count, HEADS, HEAD_DIM), (1, 0, 2))
    stacked = jnp.stack([keys[0], values[0]])
    start_state = (
        jnp.full((HEADS, tok_count), neg_big, jnp.float32),
        jnp.zeros((HEADS, tok_count), jnp.float32),
        jnp.zeros((HEADS, tok_count, HEAD_DIM), jnp.float32),
    )
    first_state = attend_piece(start_state, query_heads, query_pos, stacked, my_index * tok_count)

    def advance(offset, loop_carry):
        softmax_state, travelling = loop_carry
        travelling = passed_along(travelling, "ctx", 1)

        def compute(current):
            return attend_piece(
                current, query_heads, query_pos, travelling, (my_index - offset) * tok_count
            )

        def unchanged(current):
            return current

        softmax_state = lax.cond(offset <= my_index, compute, unchanged, softmax_state)
        return (softmax_state, travelling)

    final_state, leftover = lax.fori_loop(1, lax.axis_size("ctx"), advance, (first_state, stacked))
    run_max, run_sum, run_acc = final_state
    attended_heads = (run_acc / run_sum[:, :, None]).astype(jnp.bfloat16)
    attended = jnp.transpose(attended_heads, (1, 0, 2)).reshape(tok_count, HEADS * HEAD_DIM)
    hidden = residual[0].astype(jnp.float32) + jnp.dot(
        attended, out_proj, preferred_element_type=jnp.float32
    )
    mean_square = jnp.mean(hidden * hidden, axis=-1, keepdims=True)
    normed = (hidden * lax.rsqrt(mean_square + 1e-05) * norm_gain).astype(jnp.bfloat16)
    owners = lax.axis_size("exp")
    capacity = 3 * tok_count * TOP // (2 * owners)
    chosen = routes[0].reshape(-1)
    one_hot = (chosen[:, None] == jnp.arange(owners, dtype=jnp.int32)[None, :]).astype(jnp.int32)
    earlier = jnp.cumsum(one_hot, axis=0) - one_hot
    slot_index = jnp.sum(earlier * one_hot, axis=1)
    target = chosen * capacity + slot_index
    token_index = jnp.arange(tok_count * TOP, dtype=jnp.int32) // TOP
    slot_token = jnp.full((owners * capacity,), tok_count, jnp.int32).at[target].set(token_index)
    padded = jnp.concatenate([normed, jnp.zeros((1, normed.shape[1]), jnp.bfloat16)], axis=0)
    outgoing = padded[slot_token].reshape(owners, capacity, normed.shape[1])
    incoming = lax.all_to_all(outgoing, "exp", split_axis=0, concat_axis=0, tiled=True)
    sources, item_count, feature_width = incoming.shape
    flat_rows = incoming.reshape(sources * item_count, feature_width)
    gate_part = jnp.dot(flat_rows, w_gate[0], preferred_element_type=jnp.float32)
    up_part = jnp.dot(flat_rows, w_up[0], preferred_element_type=jnp.float32)
    activated = (jax.nn.silu(gate_part) * up_part).astype(jnp.bfloat16)
    produced = jnp.dot(activated, w_down[0], preferred_element_type=jnp.float32).astype(
        jnp.bfloat16
    )
    produced = produced.reshape(sources, item_count, feature_width)
    returned = lax.all_to_all(produced, "exp", split_axis=0, concat_axis=0, tiled=True)
    picked = (
        returned.reshape(owners * capacity, -1)[target]
        .astype(jnp.float32)
        .reshape(tok_count, TOP, -1)
    )
    mixture = jnp.sum(route_prob[0][:, :, None] * picked, axis=1)
    return (hidden + mixture).astype(jnp.bfloat16)[None]


def solution(mesh):
    placed = (
        P("exp", "ctx", None),
        P("exp", "ctx", None),
        P("exp", "ctx", None),
        P("exp", "ctx", None),
        P(),
        P(),
        P("exp", None, None),
        P("exp", None, None),
        P("exp", None, None),
        P("exp", "ctx", None),
        P("exp", "ctx", None),
    )
    return jax.shard_map(
        local, mesh=mesh, in_specs=placed, out_specs=P("exp", "ctx", None), check_vma=False
    )
```

profile of v0, /device:TPU:0, one launch (start us, length us, event | category | flops | bytes accessed | tf_op | source)
XLA Modules:
  0.0 114.4 jit_solution(14567893242107218371)
XLA Ops:
  0.0 0.9 copy.28
  2.5 0.9 copy.35
  3.4 0.9 copy.36
  4.7 1.0 pad_maximum_fusion
  6.0 28.9 %while.20 = (s32[]{:T(128)}, f32[8,64]{1,0:T(8,128)S(1)}, f32[8,64]{1,0:T(8,128)S(1)}, f32[8,64,128]{2,1,0:T(8,128)S(1)}, bf16[2,64,1024]{2,1,0:T(8,128)(2,1)S(1...) while((s32[]{:T(128)}, f32[8,64]{1,0:T(8,128)S(1)}, ...), condition=%wide.region_7.8_spmd.clone, body=%wide.region_2.7_spmd.clone.sunk | while | flops 17241732 | bytes 3983155 | solution.py:74
  6.0 5.1 %collective-permute-start = (bf16[2,64,1024]{2,1,0:T(8,128)(2,1)S(1)}, bf16[2,64,1024]{2,1,0:T(8,128)(2,1)S(1)}, u32[]{:S(2)}, u32[]{:S(2)}) collective-permute-start(bf16[2,64,1024]{2,1,0:T(8,128)(2,1)S(1)} %get-tuple-element.323), channel_id=1, source_target_pairs={{0,8},{8,16},{16,24},{1,9},{9,17},{17,25},{2,10},{10,18},{18,26},{... | collective-permute-start | bytes 786440 | tf_op jit(solution)/shard_map/while/body/eval_jaxpr/ppermute | solution.py:17
  11.1 5.5 %collective-permute-done = bf16[2,64,1024]{2,1,0:T(8,128)(2,1)S(1)} collective-permute-done((bf16[2,64,1024]{2,1,0:T(8,128)(2,1)S(1)}, bf16[2,64,1024]{2,1,0:T(8,128)(2,1)S(1)}, u32[]{:S(2)}, u32[]{:S(2)}) %collective-permute-start) | collective-permute-done | bytes 262176 | tf_op jit(solution)/shard_map/while/body/eval_jaxpr/ppermute | solution.py:17
  16.7 5.2 %collective-permute-start = (bf16[2,64,1024]{2,1,0:T(8,128)(2,1)S(1)}, bf16[2,64,1024]{2,1,0:T(8,128)(2,1)S(1)}, u32[]{:S(2)}, u32[]{:S(2)}) collective-permute-start(bf16[2,64,1024]{2,1,0:T(8,128)(2,1)S(1)} %get-tuple-element.323), channel_id=1, source_target_pairs={{0,8},{8,16},{16,24},{1,9},{9,17},{17,25},{2,10},{10,18},{18,26},{... | collective-permute-start | bytes 786440 | tf_op jit(solution)/shard_map/while/body/eval_jaxpr/ppermute | solution.py:17
  21.9 4.6 %collective-permute-done = bf16[2,64,1024]{2,1,0:T(8,128)(2,1)S(1)} collective-permute-done((bf16[2,64,1024]{2,1,0:T(8,128)(2,1)S(1)}, bf16[2,64,1024]{2,1,0:T(8,128)(2,1)S(1)}, u32[]{:S(2)}, u32[]{:S(2)}) %collective-permute-start) | collective-permute-done | bytes 262176 | tf_op jit(solution)/shard_map/while/body/eval_jaxpr/ppermute | solution.py:17
  26.6 4.4 %collective-permute-start = (bf16[2,64,1024]{2,1,0:T(8,128)(2,1)S(1)}, bf16[2,64,1024]{2,1,0:T(8,128)(2,1)S(1)}, u32[]{:S(2)}, u32[]{:S(2)}) collective-permute-start(bf16[2,64,1024]{2,1,0:T(8,128)(2,1)S(1)} %get-tuple-element.323), channel_id=1, source_target_pairs={{0,8},{8,16},{16,24},{1,9},{9,17},{17,25},{2,10},{10,18},{18,26},{... | collective-permute-start | bytes 786440 | tf_op jit(solution)/shard_map/while/body/eval_jaxpr/ppermute | solution.py:17
  31.0 3.9 %collective-permute-done = bf16[2,64,1024]{2,1,0:T(8,128)(2,1)S(1)} collective-permute-done((bf16[2,64,1024]{2,1,0:T(8,128)(2,1)S(1)}, bf16[2,64,1024]{2,1,0:T(8,128)(2,1)S(1)}, u32[]{:S(2)}, u32[]{:S(2)}) %collective-permute-start) | collective-permute-done | bytes 262176 | tf_op jit(solution)/shard_map/while/body/eval_jaxpr/ppermute | solution.py:17
  34.9 3.2 %multiply_reduce_fusion.1 = (f32[64]{0:T(128)S(1)}, f32[64,2048]{1,0:T(8,128)S(1)}) fusion(bf16[1024,2048]{1,0:T(8,128)(2,1)} %param.19, bf16[1,64,2048]{2,1,0:T(8,128)(2,1)S(1)} %copy-done.3, f32[8,64,128]{2,1,0:T(8,128)S(1)} %get-tuple-element.184, f32[8,64]{1,0:T(8,128)S(1)} %get-tuple-element.185), kind=kOutput, calls=%fused_computation.43 | convolution fusion | flops 269090752 | bytes 5245184 | tf_op jit(solution)/shard_map/dot_general | solution.py:78
  39.3 1.6 %scatter_custom_fusion = s32[384]{0:T(512)S(1)} fusion(s32[256]{0:T(256)S(1)} %bitcast.81, s32[256]{0:T(256)} %and_select_fusion, s32[]{:T(128)} %constant.41.clone.1), kind=kCustom, calls=%fused_computation.79 | custom fusion | bytes 2048 | tf_op jit(solution)/shard_map/scatter | solution.py:91
  41.0 3.1 %gather_fusion = bf16[384,2048]{1,0:T(8,128)(2,1)} fusion(bf16[65,2048]{1,0:T(8,128)(2,1)S(1)} %concatenate.3, s32[1024]{0:T(1024)S(1)} %pad_clamp_fusion.1), kind=kCustom, calls=%fused_computation | custom fusion | bytes 3147264 | tf_op jit(solution)/shard_map/gather | solution.py:93
  44.2 24.8 %all_to_all.10 = bf16[8,48,2048]{2,1,0:T(8,128)(2,1)S(1)} all-to-all(bf16[8,48,2048]{2,1,0:T(8,128)(2,1)} %bitcast.70), channel_id=1, replica_groups=mesh['ctx'=4,'exp'=8] {'exp'}, dimensions={0} | all-to-all | bytes 3145728 | tf_op jit(solution)/shard_map/all_to_all | solution.py:94
  69.0 1.1 copy-done.1
  70.2 1.9 %fusion.16 = f32[384,512]{1,0:T(8,128)} fusion(bf16[384,2048]{1,0:T(8,128)(2,1)S(1)} %bitcast.72, bf16[1,2048,512]{2,1,0:T(8,128)(2,1)S(1)} %copy-done.6), kind=kOutput, calls=%fused_computation.29 | convolution fusion | flops 805306368 | bytes 4456448 | tf_op jit(solution)/shard_map/dot_general | solution.py:97
  72.0 5.3 %convolution_convert_fusion = bf16[384,2048]{1,0:T(8,128)(2,1)} fusion(bf16[1,512,2048]{2,1,0:T(8,128)(2,1)S(1)} %copy-done, bf16[384,2048]{1,0:T(8,128)(2,1)} %bitcast.73, bf16[1,2048,512]{2,1,0:T(8,128)(2,1)} %param.22, f32[384,512]{1,0:T(8,128)} %fusion.16), kind=kOutput, calls=%fused_computation.24 | convolution fusion | flops 1612578816 | bytes 8126464 | tf_op jit(solution)/shard_map/dot_general | solution.py:100
  77.3 4.4 %all-to-all-start.1 = ((bf16[8,48,2048]{2,1,0:T(8,128)(2,1)}), bf16[8,48,2048]{2,1,0:T(8,128)(2,1)}, u32[]{:S(2)}, u32[]{:S(2)}) async-start(bf16[8,48,2048]{2,1,0:T(8,128)(2,1)} %bitcast.71), calls=%async_computation.1 | async-start | bytes 3145728 | tf_op jit(solution)/shard_map/all_to_all | solution.py:104
  81.9 20.9 %all-to-all-done.1 = bf16[8,48,2048]{2,1,0:T(8,128)(2,1)} async-done(((bf16[8,48,2048]{2,1,0:T(8,128)(2,1)}), bf16[8,48,2048]{2,1,0:T(8,128)(2,1)}, u32[]{:S(2)}, u32[]{:S(2)}) %all-to-all-start.1) | async-done | bytes 1572896 | tf_op jit(solution)/shard_map/all_to_all | solution.py:104
  102.8 5.0 %gather_fusion.1 = bf16[256,2048]{1,0:T(8,128)(2,1)} fusion(bf16[384,2048]{1,0:T(8,128)(2,1)} %bitcast.14, s32[1024]{0:T(1024)S(1)} %pad_clamp_fusion), kind=kCustom, calls=%fused_computation.1 | custom fusion | bytes 2098176 | tf_op jit(solution)/shard_map/gather | solution.py:106
  107.7 2.7 %reshape.159 = f32[64,4,2048]{2,1,0:T(4,128)} reshape(bf16[256,2048]{1,0:T(8,128)(2,1)} %gather_fusion.1) | data formatting | bytes 3145728 | tf_op jit(solution)/shard_map/convert_element_type | solution.py:107
  110.5 3.2 %multiply_reduce_fusion = f32[64,2048]{1,0:T(8,128)S(1)} fusion(f32[64,4,2048]{2,1,0:T(4,128)} %reshape.159, f32[64,4]{1,0:T(8,128)S(1)} %copy.26), kind=kLoop, calls=%fused_computation.31 | loop fusion | flops 917504 | bytes 2622464 | tf_op jit(solution)/shard_map/reduce_sum | solution.py:110
  113.7 0.8 fusion.32
  (51 shorter events, 3.6 us)
Async XLA Ops:
  0.0 72.0 %copy-start = (bf16[1,512,2048]{2,1,0:T(8,128)(2,1)S(1)}, bf16[1,512,2048]{2,1,0:T(8,128)(2,1)}, u32[]{:S(2)}) copy-start(bf16[1,512,2048]{2,1,0:T(8,128)(2,1)} %param.23) | copy-start | bytes 6291460
  0.0 5.7 %copy-start.2 = (bf16[1,64,1024]{2,1,0:T(8,128)(2,1)S(1)}, bf16[1,64,1024]{2,1,0:T(8,128)(2,1)}, u32[]{:S(2)}) copy-start(bf16[1,64,1024]{2,1,0:T(8,128)(2,1)} %param.17) | copy-start | bytes 393220
  6.0 28.9 %copy-start.3 = (bf16[1,64,2048]{2,1,0:T(8,128)(2,1)S(1)}, bf16[1,64,2048]{2,1,0:T(8,128)(2,1)}, u32[]{:S(2)}) copy-start(bf16[1,64,2048]{2,1,0:T(8,128)(2,1)} %param.18) | copy-start | bytes 786436
  6.0 10.6 %collective-permute-start = (bf16[2,64,1024]{2,1,0:T(8,128)(2,1)S(1)}, bf16[2,64,1024]{2,1,0:T(8,128)(2,1)S(1)}, u32[]{:S(2)}, u32[]{:S(2)}) collective-permute-start(bf16[2,64,1024]{2,1,0:T(8,128)(2,1)S(1)} %get-tuple-element.323), channel_id=1, source_target_pairs={{0,8},{8,16},{16,24},{1,9},{9,17},{17,25},{2,10},{10,18},{18,26},{... | collective-permute-start | bytes 786440 | tf_op jit(solution)/shard_map/while/body/eval_jaxpr/ppermute | solution.py:17
  16.7 9.9 %collective-permute-start = (bf16[2,64,1024]{2,1,0:T(8,128)(2,1)S(1)}, bf16[2,64,1024]{2,1,0:T(8,128)(2,1)S(1)}, u32[]{:S(2)}, u32[]{:S(2)}) collective-permute-start(bf16[2,64,1024]{2,1,0:T(8,128)(2,1)S(1)} %get-tuple-element.323), channel_id=1, source_target_pairs={{0,8},{8,16},{16,24},{1,9},{9,17},{17,25},{2,10},{10,18},{18,26},{... | collective-permute-start | bytes 786440 | tf_op jit(solution)/shard_map/while/body/eval_jaxpr/ppermute | solution.py:17
  26.6 8.3 %collective-permute-start = (bf16[2,64,1024]{2,1,0:T(8,128)(2,1)S(1)}, bf16[2,64,1024]{2,1,0:T(8,128)(2,1)S(1)}, u32[]{:S(2)}, u32[]{:S(2)}) collective-permute-start(bf16[2,64,1024]{2,1,0:T(8,128)(2,1)S(1)} %get-tuple-element.323), channel_id=1, source_target_pairs={{0,8},{8,16},{16,24},{1,9},{9,17},{17,25},{2,10},{10,18},{18,26},{... | collective-permute-start | bytes 786440 | tf_op jit(solution)/shard_map/while/body/eval_jaxpr/ppermute | solution.py:17
  34.9 6.0 %copy-start.4 = (f32[2048]{0:T(1024)S(1)}, f32[2048]{0:T(1024)}, u32[]{:S(2)}) copy-start(f32[2048]{0:T(1024)} %param.20) | copy-start | bytes 24580
  44.2 26.0 %copy-start.6 = (bf16[1,2048,512]{2,1,0:T(8,128)(2,1)S(1)}, bf16[1,2048,512]{2,1,0:T(8,128)(2,1)}, u32[]{:S(2)}) copy-start(bf16[1,2048,512]{2,1,0:T(8,128)(2,1)} %param.21) | copy-start | bytes 6291460
  69.0 1.1 %copy-start.1 = (bf16[8,48,2048]{2,1,0:T(8,128)(2,1)}, bf16[8,48,2048]{2,1,0:T(8,128)(2,1)S(1)}, u32[]{:S(2)}) copy-start(bf16[8,48,2048]{2,1,0:T(8,128)(2,1)S(1)} %all_to_all.10) | copy-start | bytes 4718596
  77.3 4.4 %copy-start.5 = (f32[1,64,4]{1,2,0:T(4,128)S(1)}, f32[1,64,4]{1,2,0:T(4,128)}, u32[]{:S(2)}) copy-start(f32[1,64,4]{1,2,0:T(4,128)} %param.25) | copy-start | bytes 3076
  77.3 25.5 %all-to-all-start.1 = ((bf16[8,48,2048]{2,1,0:T(8,128)(2,1)}), bf16[8,48,2048]{2,1,0:T(8,128)(2,1)}, u32[]{:S(2)}, u32[]{:S(2)}) async-start(bf16[8,48,2048]{2,1,0:T(8,128)(2,1)} %bitcast.71), calls=%async_computation.1 | async-start | bytes 3145728 | tf_op jit(solution)/shard_map/all_to_all | solution.py:104
where the time goes:
time: 116 us; the launch traced here: 114 us
  waiting for transfers between devices  34.9 us (30%)
  blocking collectives  24.8 us (21%)
  starting transfers between devices  19.1 us (16%)
  local copies, waits for them, and re-layouts  17.2 us (15%)
  matrix products  10.8 us (9%)
  other arithmetic  7.24 us (6%)
    all_to_all x1, blocking collectives, local(): lax.all_to_all(outgoing, 'exp', split_axis=0, concat_axis=0, tiled=True)  24.8 us
    all_to_all x1, waiting for transfers between devices, local(): lax.all_to_all(produced, 'exp', split_axis=0, concat_axis=0, tiled=True)  20.9 us
    ppermute x3, starting transfers between devices, passed_along(): return lax.ppermute(block, axis, route)  14.7 us
    ppermute x3, waiting for transfers between devices, passed_along(): return lax.ppermute(block, axis, route)  14 us
    dot_general x1, matrix products, local(): jnp.dot(activated, w_down[0], preferred_element_type=jnp.float32)  5.3 us
    gather x1, local copies, waits for them, and re-layouts, local(): returned.reshape(owners * capacity, -1)[target].astype(jnp.float32)  4.96 us
    all_to_all x1, starting transfers between devices, local(): lax.all_to_all(produced, 'exp', split_axis=0, concat_axis=0, tiled=True)  4.42 us
    unnamed x18, local copies, waits for them, and re-layouts  3.98 us
  transfers between devices with their start and end apart: 4, of which 4 were waited for; matrix products, arithmetic and copies ran while one was open for 0% of the time, Pallas kernels for 0%

commit v1 on v0

--- a/solution.py
+++ b/solution.py
@@ -1,6 +1,10 @@
+import functools
+
 import jax
 import jax.numpy as jnp
 from jax import lax
+from jax.experimental import pallas as pl
+from jax.experimental.pallas import tpu as pltpu
 from jax.sharding import PartitionSpec as P
 
 HEADS = 8
@@ -111,6 +115,240 @@
     return (hidden + mixture).astype(jnp.bfloat16)[None]
 
 
+MESH = pl.DeviceIdType.MESH
+
+
+def fused_kernel(
+    n, chips, q_hbm, k_hbm, v_hbm, res_hbm, wo_hbm, gain_ref, wg_hbm, wu_hbm, wd_hbm, routes_ref, prob_ref,
+    out_ref,
+    qkv, att, attg, resg, probg, wo, wg, wu, wd, kept, hidden, own, psend, precv, ssend, srecv,
+    load_sem, qkv_s, qkv_r, back_s, back_r, near_s, near_r, fwd_s, fwd_r, pair_s, pair_r, sum_s, sum_r,
+):
+    z = lax.axis_index("ctx")
+    me = lax.axis_index("exp")
+    core = lax.rem(me, 2)
+    chip = me // 2
+    partner = me + 1 - 2 * core
+    toks = q_hbm.shape[1]
+    width = qkv.shape[-1]
+    heads_here = width // HEAD_DIM
+
+    def across(d):
+        there = chip
+        for b in range(chips.bit_length() - 1):
+            if (d >> b) & 1:
+                there = there + (1 << b) * (1 - 2 * lax.rem(chip // (1 << b), 2))
+        return 2 * there + core
+
+    def remote(src, dst, ssem, rsem, **to):
+        return pltpu.make_async_remote_copy(
+            src_ref=src, dst_ref=dst, send_sem=ssem, recv_sem=rsem, device_id=to, device_id_type=MESH
+        )
+
+    def columns(j):
+        return pl.ds(pl.multiple_of(j * width, width), width)
+
+    sources = (q_hbm, k_hbm, v_hbm)
+    started = []
+
+    def go(copy):
+        copy.start()
+        started.append(copy)
+        return copy
+
+    own_qkv = []
+    for t in range(3):
+        own_qkv.append(pltpu.make_async_copy(sources[t].at[0, :, columns(z)], qkv.at[t, z], load_sem.at[t]))
+        own_qkv[-1].start()
+    own_res = pltpu.make_async_copy(res_hbm.at[0], resg.at[0, 0], load_sem.at[3])
+    own_res.start()
+    loads = []
+    for i, (src, dst) in enumerate(((wo_hbm, wo), (wg_hbm.at[0], wg), (wu_hbm.at[0], wu), (wd_hbm.at[0], wd))):
+        loads.append(pltpu.make_async_copy(src, dst, load_sem.at[4 + i]))
+        loads[-1].start()
+
+    barrier = pltpu.get_barrier_semaphore()
+    for d in range(1, n):
+        pl.semaphore_signal(barrier, inc=1, device_id={"ctx": lax.rem(z + d, n)}, device_id_type=MESH)
+    for d in range(1, chips):
+        pl.semaphore_signal(barrier, inc=1, device_id={"exp": across(d)}, device_id_type=MESH)
+    pl.semaphore_signal(barrier, inc=1, device_id={"exp": partner}, device_id_type=MESH)
+    pl.semaphore_wait(barrier, n - 1 + chips)
+
+    for t in range(3):
+        for d in range(1, n):
+            j = lax.rem(z + d, n)
+            go(remote(sources[t].at[0, :, columns(j)], qkv.at[t, z], qkv_s.at[t, j], qkv_r.at[t, z], ctx=j))
+    go(remote(res_hbm.at[0], resg.at[0, 1], near_s.at[0, 0], near_r.at[0, 0], exp=partner))
+    for d in range(1, chips):
+        go(remote(res_hbm.at[0], resg.at[d, 0], near_s.at[0, d], near_r.at[0, d], exp=across(d)))
+    lanes = lax.broadcasted_iota(jnp.int32, probg.shape[2:], 1)
+    dense = jnp.zeros(probg.shape[2:], jnp.float32)
+    for t in range(TOP):
+        dense = dense + jnp.where(lanes == routes_ref[0, :, t : t + 1], prob_ref[0, :, t : t + 1], 0.0)
+    probg[0, 0] = dense
+    go(remote(probg.at[0, 0], probg.at[0, 1], near_s.at[1, 0], near_r.at[1, 0], exp=partner))
+    for d in range(1, chips):
+        go(remote(probg.at[0, 0], probg.at[d, 0], near_s.at[1, d], near_r.at[1, d], exp=across(d)))
+
+    for t in range(3):
+        own_qkv[t].wait()
+        for d in range(1, n):
+            s = lax.rem(z + d, n)
+            remote(qkv.at[t, s], qkv.at[t, s], qkv_s.at[t, s], qkv_r.at[t, s], ctx=s).wait_recv()
+    length = n * toks
+    row = lax.broadcasted_iota(jnp.int32, (length, length), 0)
+    col = lax.broadcasted_iota(jnp.int32, (length, length), 1)
+    for h in range(heads_here):
+        part = slice(h * HEAD_DIM, (h + 1) * HEAD_DIM)
+        qh = qkv[0, :, :, part].reshape(length, HEAD_DIM)
+        kh = qkv[1, :, :, part].reshape(length, HEAD_DIM)
+        vh = qkv[2, :, :, part].reshape(length, HEAD_DIM)
+        scores = lax.dot_general(qh, kh, (((1,), (1,)), ((), ())), preferred_element_type=jnp.float32)
+        scores = jnp.where(col <= row, scores * HEAD_DIM ** (-0.5), neg_big)
+        expo = jnp.exp(scores - jnp.max(scores, axis=1, keepdims=True))
+        expo = jnp.where(col <= row, expo, 0.0)
+        denom = jnp.sum(expo, axis=1, keepdims=True)
+        mixed = jnp.dot(expo.astype(jnp.bfloat16), vh, preferred_element_type=jnp.float32) / denom
+        att[:, :, part] = mixed.astype(jnp.bfloat16).reshape(n, toks, HEAD_DIM)
+
+    for d in range(1, n):
+        j = lax.rem(z + d, n)
+        go(remote(att.at[j], attg.at[0, 0, :, columns(z)], back_s.at[j], back_r.at[z], ctx=j))
+    own_att = pltpu.make_async_copy(att.at[z], attg.at[0, 0, :, columns(z)], load_sem.at[8])
+    own_att.start()
+    own_att.wait()
+    for d in range(1, n):
+        s = lax.rem(z + d, n)
+        here = attg.at[0, 0, :, columns(s)]
+        remote(att.at[s], here, back_s.at[s], back_r.at[s], ctx=s).wait_recv()
+
+    go(remote(attg.at[0, 0], attg.at[0, 1], near_s.at[2, 0], near_r.at[2, 0], exp=partner))
+    for d in range(1, chips):
+        go(remote(attg.at[0, 0], attg.at[d, 0], near_s.at[2, d], near_r.at[2, d], exp=across(d)))
+
+    kinds = (resg, probg, attg)
+
+    def arrived(kind, d, half):
+        buf = kinds[kind]
+        if half == 0 or d == 0:
+            sems = near_s.at[kind, d], near_r.at[kind, d]
+        else:
+            sems = fwd_s.at[kind, d], fwd_r.at[kind, d]
+        remote(buf.at[d, half], buf.at[d, half], *sems, exp=partner).wait_recv()
+
+    def forward(kind, d):
+        arrived(kind, d, 0)
+        buf = kinds[kind]
+        go(remote(buf.at[d, 0], buf.at[d, 1], fwd_s.at[kind, d], fwd_r.at[kind, d], exp=partner))
+
+    for d in range(1, chips):
+        forward(0, d)
+        forward(1, d)
+    own_res.wait()
+    for copy in loads:
+        copy.wait()
+    gain = gain_ref[...]
+
+    def project(d):
+        for kind in (0, 1, 2):
+            arrived(kind, d, 1)
+        rows = attg[d].reshape(2 * toks, -1)
+        res = resg[d].reshape(2 * toks, -1).astype(jnp.float32)
+        hidden[...] = res + jnp.dot(rows, wo[...], preferred_element_type=jnp.float32)
+
+    def experts(d):
+        state = hidden[...]
+        mean_square = jnp.mean(state * state, axis=-1, keepdims=True)
+        normed = (state * lax.rsqrt(mean_square + 1e-05) * gain).astype(jnp.bfloat16)
+        gate = jnp.dot(normed, wg[...], preferred_element_type=jnp.float32)
+        up = jnp.dot(normed, wu[...], preferred_element_type=jnp.float32)
+        act = (gate / (1.0 + jnp.exp(-gate)) * up).astype(jnp.bfloat16)
+        made = jnp.dot(act, wd[...], preferred_element_type=jnp.float32)
+        share = probg[d].reshape(2 * toks, -1)
+        lane = lax.broadcasted_iota(jnp.int32, share.shape, 1)
+        weight = jnp.sum(jnp.where(lane == me, share, 0.0), axis=-1, keepdims=True)
+        made = made * weight
+        psend[d] = made[toks:].astype(jnp.bfloat16)
+        go(remote(psend.at[d], precv.at[d], pair_s.at[d], pair_r.at[d], exp=partner))
+        return made[:toks]
+
+    def from_partner(d):
+        remote(psend.at[d], precv.at[d], pair_s.at[d], pair_r.at[d], exp=partner).wait_recv()
+        return precv[d].astype(jnp.float32)
+
+    def give_back(d):
+        ssend[d] = (kept[...] + from_partner(d)).astype(jnp.bfloat16)
+        go(remote(ssend.at[d], srecv.at[d], sum_s.at[d], sum_r.at[d], exp=across(d)))
+
+    project(0)
+    own[...] = hidden[:toks] + experts(0)
+    for d in range(1, chips):
+        forward(2, d)
+        project(d)
+        if d > 1:
+            give_back(d - 1)
+        kept[...] = experts(d)
+    give_back(chips - 1)
+    total = own[...] + from_partner(0)
+    for d in range(1, chips):
+        remote(ssend.at[d], srecv.at[d], sum_s.at[d], sum_r.at[d], exp=partner).wait_recv()
+        total = total + srecv[d].astype(jnp.float32)
+    out_ref[0] = total.astype(jnp.bfloat16)
+    for copy in started:
+        copy.wait_send()
+
+
+def fused(
+    n, owners, queries, keys, values, residual, out_proj, norm_gain, w_gate, w_up, w_down, routes, route_prob
+):
+    chips = owners // 2
+    toks, depth = queries.shape[1:]
+    model, ffw = w_gate.shape[1:]
+    width = depth // n
+    lanes = -(-owners // 128) * 128
+    bf16, f32 = jnp.bfloat16, jnp.float32
+    whole, hbm = pl.BlockSpec(memory_space=pltpu.VMEM), pl.BlockSpec(memory_space=pl.ANY)
+    dma = pltpu.SemaphoreType.DMA
+    return pl.pallas_call(
+        functools.partial(fused_kernel, n, chips),
+        out_shape=jax.ShapeDtypeStruct((1, toks, model), bf16),
+        in_specs=[hbm, hbm, hbm, hbm, hbm, whole, hbm, hbm, hbm, whole, whole],
+        out_specs=whole,
+        scratch_shapes=[
+            pltpu.VMEM((3, n, toks, width), bf16),
+            pltpu.VMEM((n, toks, width), bf16),
+            pltpu.VMEM((chips, 2, toks, depth), bf16),
+            pltpu.VMEM((chips, 2, toks, model), bf16),
+            pltpu.VMEM((chips, 2, toks, lanes), f32),
+            pltpu.VMEM((depth, model), bf16),
+            pltpu.VMEM((model, ffw), bf16),
+            pltpu.VMEM((model, ffw), bf16),
+            pltpu.VMEM((ffw, model), bf16),
+            pltpu.VMEM((toks, model), f32),
+            pltpu.VMEM((2 * toks, model), f32),
+            pltpu.VMEM((toks, model), f32),
+            pltpu.VMEM((chips, toks, model), bf16),
+            pltpu.VMEM((chips, toks, model), bf16),
+            pltpu.VMEM((chips, toks, model), bf16),
+            pltpu.VMEM((chips, toks, model), bf16),
+            dma((9,)),
+            dma((3, n)), dma((3, n)),
+            dma((n,)), dma((n,)),
+            dma((3, chips)), dma((3, chips)),
+            dma((3, chips)), dma((3, chips)),
+            dma((chips,)), dma((chips,)),
+            dma((chips,)), dma((chips,)),
+        ],
+        compiler_params=pltpu.CompilerParams(
+            collective_id=0, has_side_effects=True, vmem_limit_bytes=48 * 1024 * 1024
+        ),
+    )(
+        queries, keys, values, residual, out_proj, norm_gain.reshape(1, -1), w_gate, w_up, w_down,
+        routes, route_prob,
+    )
+
+
 def solution(mesh):
     placed = (
         P("exp", "ctx", None),
@@ -125,6 +363,10 @@
         P("exp", "ctx", None),
         P("exp", "ctx", None),
     )
+    n, owners = mesh.shape["ctx"], mesh.shape["exp"]
+    chips = owners // 2
+    splits = HEADS % n == 0 and owners % 2 == 0 and chips & (chips - 1) == 0
+    step = functools.partial(fused, n, owners) if splits else local
     return jax.shard_map(
-        local, mesh=mesh, in_specs=placed, out_specs=P("exp", "ctx", None), check_vma=False
-    )
+        step, mesh=mesh, in_specs=placed, out_specs=P("exp", "ctx", None), check_vma=False
+    )

time: 116 us -> 56.8 us (0.49); the launches traced: 114 us -> 56.5 us
  Pallas kernels: 0 us -> 46.7 us
  waiting for transfers between devices: 34.9 us -> 0 us
  blocking collectives: 24.8 us -> 0 us
  starting transfers between devices: 19.1 us -> 0 us
  matrix products: 10.8 us -> 0 us
  local copies, waits for them, and re-layouts: 17.2 us -> 9.78 us
  other arithmetic: 7.24 us -> 0 us
    pallas_call x0 -> x1, Pallas kernels: none -> 46.7 us  [fused(): pl.pallas_call(functools.partial(fused_kernel, n, chips), out_shape=jax.S...]
    all_to_all x1 -> x0, blocking collectives: 24.8 us -> none  [local(): lax.all_to_all(outgoing, 'exp', split_axis=0, concat_axis=0, tiled=True)]
    all_to_all x1 -> x0, waiting for transfers between devices: 20.9 us -> none  [local(): lax.all_to_all(produced, 'exp', split_axis=0, concat_axis=0, tiled=True)]
    ppermute x3 -> x0, starting transfers between devices: 14.7 us -> none  [passed_along(): return lax.ppermute(block, axis, route)]
    ppermute x3 -> x0, waiting for transfers between devices: 14 us -> none  [passed_along(): return lax.ppermute(block, axis, route)]
    dot_general x5 -> x0, matrix products: 10.8 us -> none  [the longest x1 5.3 us: local(): jnp.dot(activated, w_down[0], preferred_element_type=jnp.float32)]
    gather x2 -> x0, local copies, waits for them, and re-layouts: 8.1 us -> none  [the longest x1 4.96 us: local(): returned.reshape(owners * capacity, -1)[target].astype(jnp.float32)]
    unnamed x18 -> x17, local copies, waits for them, and re-layouts: 3.98 us -> 9.78 us
  transfers between devices with their start and end apart: 4 -> 0, of which waited for: 4 -> 0; matrix products, arithmetic and copies ran while one was open for 0% -> 0% of each run, Pallas kernels for 0% -> 0%
where the time goes in v1:
time: 56.8 us; the launch traced here: 56.5 us
  Pallas kernels  46.7 us (82%)
  local copies, waits for them, and re-layouts  9.78 us (17%)
    pallas_call x1, Pallas kernels, fused(): pl.pallas_call(functools.partial(fused_kernel, n, chips), out_shape=jax.S...  46.7 us
    unnamed x17, local copies, waits for them, and re-layouts  9.78 us

profile of v1, /device:TPU:0, one launch (start us, length us, event | category | flops | bytes accessed | tf_op | source)
XLA Modules:
  0.0 56.5 jit_solution(12012759043865862398)
XLA Ops:
  0.0 0.8 %copy.12.routes_ref = s32[1,64,4]{2,1,0:T(8,128)S(1)} copy(s32[1,64,4]{1,2,0:T(4,128)} %param.20) | data formatting | bytes 2048 | tf_op args[9]
  0.8 0.8 %copy.13.prob_ref = f32[1,64,4]{2,1,0:T(8,128)S(1)} copy(f32[1,64,4]{1,2,0:T(4,128)} %param.21) | data formatting | bytes 2048 | tf_op args[10]
  1.5 0.0 copy-start
  1.5 1.6 %copy-done = bf16[1,2048,512]{2,1,0:T(8,128)(2,1)S(1)} copy-done((bf16[1,2048,512]{2,1,0:T(8,128)(2,1)S(1)}, bf16[1,2048,512]{2,1,0:T(8,128)(2,1)}, u32[]{:S(2)}) %copy-start) | copy-done | bytes 2097176
  3.1 0.0 copy-start.1
  3.1 1.6 %copy-done.1 = bf16[1,2048,512]{2,1,0:T(8,128)(2,1)S(1)} copy-done((bf16[1,2048,512]{2,1,0:T(8,128)(2,1)S(1)}, bf16[1,2048,512]{2,1,0:T(8,128)(2,1)}, u32[]{:S(2)}) %copy-start.1) | copy-done | bytes 2097176
  4.7 0.0 copy-start.2
  4.7 0.9 %copy-done.2 = bf16[1,64,2048]{2,1,0:T(8,128)(2,1)S(1)} copy-done((bf16[1,64,2048]{2,1,0:T(8,128)(2,1)S(1)}, bf16[1,64,2048]{2,1,0:T(8,128)(2,1)}, u32[]{:S(2)}) %copy-start.2) | copy-done | bytes 262168
  5.7 0.0 copy-start.3
  5.7 0.9 %copy-done.3 = bf16[1,64,1024]{2,1,0:T(8,128)(2,1)S(1)} copy-done((bf16[1,64,1024]{2,1,0:T(8,128)(2,1)S(1)}, bf16[1,64,1024]{2,1,0:T(8,128)(2,1)}, u32[]{:S(2)}) %copy-start.3) | copy-done | bytes 131096
  6.6 0.0 copy-start.4
  6.6 0.9 %copy-done.4 = bf16[1,64,1024]{2,1,0:T(8,128)(2,1)S(1)} copy-done((bf16[1,64,1024]{2,1,0:T(8,128)(2,1)S(1)}, bf16[1,64,1024]{2,1,0:T(8,128)(2,1)}, u32[]{:S(2)}) %copy-start.4) | copy-done | bytes 131096
  7.5 0.0 copy-start.5
  7.5 0.9 %copy-done.5 = bf16[1,64,1024]{2,1,0:T(8,128)(2,1)S(1)} copy-done((bf16[1,64,1024]{2,1,0:T(8,128)(2,1)S(1)}, bf16[1,64,1024]{2,1,0:T(8,128)(2,1)}, u32[]{:S(2)}) %copy-start.5) | copy-done | bytes 131096
  8.4 0.0 copy-start.6
  8.4 0.7 %copy-done.6 = f32[2048]{0:T(1024)S(1)} copy-done((f32[2048]{0:T(1024)S(1)}, f32[2048]{0:T(1024)}, u32[]{:S(2)}) %copy-start.6) | copy-done | bytes 8216
  9.1 46.7 %shard_map.109 = bf16[1,64,2048]{2,1,0:T(8,128)(2,1)S(1)} custom-call(bf16[1,64,1024]{2,1,0:T(8,128)(2,1)S(1)} %copy-done.3, bf16[1,64,1024]{2,1,0:T(8,128)(2,1)S(1)} %copy-done.4, bf16[1,64,1024]{2,1,0:T(8,128)(2,1)S(1)} %copy-done.5, bf16[1,64,2048]{2,1,0:T(8,128)(2,1)S(1)} %copy-done.2, bf16[1024,2048]{1,0:T(8,128)(2,1)} %wo_hbm.1, ...), custom_call_target="tpu_custom_call" | custom-call | tf_op jit(solution)/shard_map/pallas_call | solution.py:313
  55.7 0.7 %copy.15 = bf16[1,64,2048]{2,1,0:T(8,128)(2,1)} copy(bf16[1,64,2048]{2,1,0:T(8,128)(2,1)S(1)} %shard_map.109) | data formatting | bytes 524288
Async XLA Ops:
  1.5 1.6 %copy-start = (bf16[1,2048,512]{2,1,0:T(8,128)(2,1)S(1)}, bf16[1,2048,512]{2,1,0:T(8,128)(2,1)}, u32[]{:S(2)}) copy-start(bf16[1,2048,512]{2,1,0:T(8,128)(2,1)} %wg_hbm.1) | copy-start | bytes 6291460
  3.1 1.6 %copy-start.1 = (bf16[1,2048,512]{2,1,0:T(8,128)(2,1)S(1)}, bf16[1,2048,512]{2,1,0:T(8,128)(2,1)}, u32[]{:S(2)}) copy-start(bf16[1,2048,512]{2,1,0:T(8,128)(2,1)} %wu_hbm.1) | copy-start | bytes 6291460
  4.7 0.9 %copy-start.2 = (bf16[1,64,2048]{2,1,0:T(8,128)(2,1)S(1)}, bf16[1,64,2048]{2,1,0:T(8,128)(2,1)}, u32[]{:S(2)}) copy-start(bf16[1,64,2048]{2,1,0:T(8,128)(2,1)} %res_hbm.1) | copy-start | bytes 786436
  5.7 0.9 %copy-start.3 = (bf16[1,64,1024]{2,1,0:T(8,128)(2,1)S(1)}, bf16[1,64,1024]{2,1,0:T(8,128)(2,1)}, u32[]{:S(2)}) copy-start(bf16[1,64,1024]{2,1,0:T(8,128)(2,1)} %q_hbm.1) | copy-start | bytes 393220
  6.6 0.9 %copy-start.4 = (bf16[1,64,1024]{2,1,0:T(8,128)(2,1)S(1)}, bf16[1,64,1024]{2,1,0:T(8,128)(2,1)}, u32[]{:S(2)}) copy-start(bf16[1,64,1024]{2,1,0:T(8,128)(2,1)} %k_hbm.1) | copy-start | bytes 393220
  7.5 0.9 %copy-start.5 = (bf16[1,64,1024]{2,1,0:T(8,128)(2,1)S(1)}, bf16[1,64,1024]{2,1,0:T(8,128)(2,1)}, u32[]{:S(2)}) copy-start(bf16[1,64,1024]{2,1,0:T(8,128)(2,1)} %v_hbm.1) | copy-start | bytes 393220
  8.4 0.7 %copy-start.6 = (f32[2048]{0:T(1024)S(1)}, f32[2048]{0:T(1024)}, u32[]{:S(2)}) copy-start(f32[2048]{0:T(1024)} %param.16) | copy-start | bytes 24580

commit v2 on v1

--- a/solution.py
+++ b/solution.py
@@ -122,7 +122,7 @@
     n, chips, q_hbm, k_hbm, v_hbm, res_hbm, wo_hbm, gain_ref, wg_hbm, wu_hbm, wd_hbm, routes_ref, prob_ref,
     out_ref,
     qkv, att, attg, resg, probg, wo, wg, wu, wd, kept, hidden, own, psend, precv, ssend, srecv,
-    load_sem, qkv_s, qkv_r, back_s, back_r, near_s, near_r, fwd_s, fwd_r, pair_s, pair_r, sum_s, sum_r,
+    load_sem, qkv_s, qkv_r, back_s, back_r, att_s, att_r, near_s, near_r, fwd_s, fwd_r, pair_s, pair_r, sum_s, sum_r,
 ):
     z = lax.axis_index("ctx")
     me = lax.axis_index("exp")
@@ -191,46 +191,61 @@
     for d in range(1, chips):
         go(remote(probg.at[0, 0], probg.at[d, 0], near_s.at[1, d], near_r.at[1, d], exp=across(d)))
 
-    for t in range(3):
+    def collected(t):
         own_qkv[t].wait()
         for d in range(1, n):
             s = lax.rem(z + d, n)
             remote(qkv.at[t, s], qkv.at[t, s], qkv_s.at[t, s], qkv_r.at[t, s], ctx=s).wait_recv()
+
+    collected(0)
+    collected(1)
     length = n * toks
     row = lax.broadcasted_iota(jnp.int32, (length, length), 0)
     col = lax.broadcasted_iota(jnp.int32, (length, length), 1)
-    for h in range(heads_here):
-        part = slice(h * HEAD_DIM, (h + 1) * HEAD_DIM)
+    parts = [slice(h * HEAD_DIM, (h + 1) * HEAD_DIM) for h in range(heads_here)]
+    soft = []
+    for part in parts:
         qh = qkv[0, :, :, part].reshape(length, HEAD_DIM)
         kh = qkv[1, :, :, part].reshape(length, HEAD_DIM)
-        vh = qkv[2, :, :, part].reshape(length, HEAD_DIM)
         scores = lax.dot_general(qh, kh, (((1,), (1,)), ((), ())), preferred_element_type=jnp.float32)
         scores = jnp.where(col <= row, scores * HEAD_DIM ** (-0.5), neg_big)
         expo = jnp.exp(scores - jnp.max(scores, axis=1, keepdims=True))
         expo = jnp.where(col <= row, expo, 0.0)
-        denom = jnp.sum(expo, axis=1, keepdims=True)
-        mixed = jnp.dot(expo.astype(jnp.bfloat16), vh, preferred_element_type=jnp.float32) / denom
+        soft.append((expo.astype(jnp.bfloat16), jnp.sum(expo, axis=1, keepdims=True)))
+    collected(2)
+    for part, (expo, denom) in zip(parts, soft):
+        vh = qkv[2, :, :, part].reshape(length, HEAD_DIM)
+        mixed = jnp.dot(expo, vh, preferred_element_type=jnp.float32) / denom
         att[:, :, part] = mixed.astype(jnp.bfloat16).reshape(n, toks, HEAD_DIM)
+
+    def share(src, s):
+        go(remote(src, attg.at[0, 1, :, columns(s)], att_s.at[s, 0], att_r.at[s, 0], exp=partner))
+        for d in range(1, chips):
+            go(remote(src, attg.at[d, 0, :, columns(s)], att_s.at[s, d], att_r.at[s, d], exp=across(d)))
 
     for d in range(1, n):
         j = lax.rem(z + d, n)
         go(remote(att.at[j], attg.at[0, 0, :, columns(z)], back_s.at[j], back_r.at[z], ctx=j))
     own_att = pltpu.make_async_copy(att.at[z], attg.at[0, 0, :, columns(z)], load_sem.at[8])
     own_att.start()
-    own_att.wait()
-    for d in range(1, n):
+    share(att.at[z], z)
+    for d in sorted(range(1, n), key=lambda d: min(d, n - d)):
         s = lax.rem(z + d, n)
         here = attg.at[0, 0, :, columns(s)]
         remote(att.at[s], here, back_s.at[s], back_r.at[s], ctx=s).wait_recv()
-
-    go(remote(attg.at[0, 0], attg.at[0, 1], near_s.at[2, 0], near_r.at[2, 0], exp=partner))
-    for d in range(1, chips):
-        go(remote(attg.at[0, 0], attg.at[d, 0], near_s.at[2, d], near_r.at[2, d], exp=across(d)))
+        share(here, s)
+    own_att.wait()
 
     kinds = (resg, probg, attg)
 
     def arrived(kind, d, half):
         buf = kinds[kind]
+        if kind == 2 and (half == 0 or d == 0):
+            for i in range(n):
+                s = lax.rem(z + i, n)
+                here = buf.at[d, half, :, columns(s)]
+                remote(here, here, att_s.at[s, d], att_r.at[s, d], exp=partner).wait_recv()
+            return
         if half == 0 or d == 0:
             sems = near_s.at[kind, d], near_r.at[kind, d]
         else:
@@ -242,55 +257,65 @@
         buf = kinds[kind]
         go(remote(buf.at[d, 0], buf.at[d, 1], fwd_s.at[kind, d], fwd_r.at[kind, d], exp=partner))
 
-    for d in range(1, chips):
-        forward(0, d)
-        forward(1, d)
     own_res.wait()
     for copy in loads:
         copy.wait()
     gain = gain_ref[...]
 
-    def project(d):
-        for kind in (0, 1, 2):
-            arrived(kind, d, 1)
-        rows = attg[d].reshape(2 * toks, -1)
-        res = resg[d].reshape(2 * toks, -1).astype(jnp.float32)
-        hidden[...] = res + jnp.dot(rows, wo[...], preferred_element_type=jnp.float32)
-
-    def experts(d):
-        state = hidden[...]
+    def project(lo, hi):
+        for d in range(lo, hi):
+            for kind in (0, 1, 2):
+                arrived(kind, d, 1)
+        count = 2 * toks * (hi - lo)
+        rows = attg[lo:hi].reshape(count, -1)
+        res = resg[lo:hi].reshape(count, -1).astype(jnp.float32)
+        hidden[:count] = res + jnp.dot(rows, wo[...], preferred_element_type=jnp.float32)
+
+    def experts(lo, hi):
+        count = 2 * toks * (hi - lo)
+        state = hidden[:count]
         mean_square = jnp.mean(state * state, axis=-1, keepdims=True)
         normed = (state * lax.rsqrt(mean_square + 1e-05) * gain).astype(jnp.bfloat16)
         gate = jnp.dot(normed, wg[...], preferred_element_type=jnp.float32)
         up = jnp.dot(normed, wu[...], preferred_element_type=jnp.float32)
         act = (gate / (1.0 + jnp.exp(-gate)) * up).astype(jnp.bfloat16)
         made = jnp.dot(act, wd[...], preferred_element_type=jnp.float32)
-        share = probg[d].reshape(2 * toks, -1)
+        share = probg[lo:hi].reshape(count, -1)
         lane = lax.broadcasted_iota(jnp.int32, share.shape, 1)
         weight = jnp.sum(jnp.where(lane == me, share, 0.0), axis=-1, keepdims=True)
-        made = made * weight
-        psend[d] = made[toks:].astype(jnp.bfloat16)
-        go(remote(psend.at[d], precv.at[d], pair_s.at[d], pair_r.at[d], exp=partner))
-        return made[:toks]
+        made = (made * weight).reshape(hi - lo, 2, toks, -1)
+        for d in range(lo, hi):
+            psend[d] = made[d - lo, 1].astype(jnp.bfloat16)
+            go(remote(psend.at[d], precv.at[d], pair_s.at[d], pair_r.at[d], exp=partner))
+        kept[lo:hi] = made[:, 0]
 
     def from_partner(d):
         remote(psend.at[d], precv.at[d], pair_s.at[d], pair_r.at[d], exp=partner).wait_recv()
         return precv[d].astype(jnp.float32)
 
     def give_back(d):
-        ssend[d] = (kept[...] + from_partner(d)).astype(jnp.bfloat16)
+        ssend[d] = (kept[d] + from_partner(d)).astype(jnp.bfloat16)
         go(remote(ssend.at[d], srecv.at[d], sum_s.at[d], sum_r.at[d], exp=across(d)))
 
-    project(0)
-    own[...] = hidden[:toks] + experts(0)
-    for d in range(1, chips):
-        forward(2, d)
-        project(d)
-        if d > 1:
-            give_back(d - 1)
-        kept[...] = experts(d)
-    give_back(chips - 1)
-    total = own[...] + from_partner(0)
+    project(0, 1)
+    own[...] = hidden[:toks]
+    for d in range(1, chips):
+        forward(0, d)
+        forward(1, d)
+    experts(0, 1)
+    before = range(0)
+    for lo in range(1, chips, 2):
+        hi = min(lo + 2, chips)
+        for d in range(lo, hi):
+            forward(2, d)
+        project(lo, hi)
+        for d in before:
+            give_back(d)
+        experts(lo, hi)
+        before = range(lo, hi)
+    for d in before:
+        give_back(d)
+    total = own[...] + kept[0] + from_partner(0)
     for d in range(1, chips):
         remote(ssend.at[d], srecv.at[d], sum_s.at[d], sum_r.at[d], exp=partner).wait_recv()
         total = total + srecv[d].astype(jnp.float32)
@@ -308,7 +333,7 @@
     width = depth // n
     lanes = -(-owners // 128) * 128
     bf16, f32 = jnp.bfloat16, jnp.float32
-    whole, hbm = pl.BlockSpec(memory_space=pltpu.VMEM), pl.BlockSpec(memory_space=pl.ANY)
+    whole, hbm = pl.BlockSpec(memory_space=pltpu.VMEM), pl.BlockSpec(memory_space=pltpu.HBM)
     dma = pltpu.SemaphoreType.DMA
     return pl.pallas_call(
         functools.partial(fused_kernel, n, chips),
@@ -325,8 +350,8 @@
             pltpu.VMEM((model, ffw), bf16),
             pltpu.VMEM((model, ffw), bf16),
             pltpu.VMEM((ffw, model), bf16),
-            pltpu.VMEM((toks, model), f32),
-            pltpu.VMEM((2 * toks, model), f32),
+            pltpu.VMEM((chips, toks, model), f32),
+            pltpu.VMEM((4 * toks, model), f32),
             pltpu.VMEM((toks, model), f32),
             pltpu.VMEM((chips, toks, model), bf16),
             pltpu.VMEM((chips, toks, model), bf16),
@@ -335,6 +360,7 @@
             dma((9,)),
             dma((3, n)), dma((3, n)),
             dma((n,)), dma((n,)),
+            dma((n, chips)), dma((n, chips)),
             dma((3, chips)), dma((3, chips)),
             dma((3, chips)), dma((3, chips)),
             dma((chips,)), dma((chips,)),

time: 56.8 us -> 56.6 us (level)
  no operation moved by 1% of the time
where the time goes in v2:
time: 56.6 us; the launch traced here: 56.2 us
  Pallas kernels  46.4 us (82%)
  local copies, waits for them, and re-layouts  9.78 us (17%)
    pallas_call x1, Pallas kernels, fused(): pl.pallas_call(functools.partial(fused_kernel, n, chips), out_shape=jax.S...  46.4 us
    unnamed x17, local copies, waits for them, and re-layouts  9.78 us

profile of v2, /device:TPU:0, one launch (start us, length us, event | category | flops | bytes accessed | tf_op | source)
XLA Modules:
  0.0 56.2 jit_solution(6543147198371088275)
XLA Ops:
  0.0 0.8 %copy.12.routes_ref = s32[1,64,4]{2,1,0:T(8,128)S(1)} copy(s32[1,64,4]{1,2,0:T(4,128)} %param.20) | data formatting | bytes 2048 | tf_op args[9]
  0.8 0.8 %copy.13.prob_ref = f32[1,64,4]{2,1,0:T(8,128)S(1)} copy(f32[1,64,4]{1,2,0:T(4,128)} %param.21) | data formatting | bytes 2048 | tf_op args[10]
  1.5 0.0 copy-start
  1.5 1.6 %copy-done = bf16[1,2048,512]{2,1,0:T(8,128)(2,1)S(1)} copy-done((bf16[1,2048,512]{2,1,0:T(8,128)(2,1)S(1)}, bf16[1,2048,512]{2,1,0:T(8,128)(2,1)}, u32[]{:S(2)}) %copy-start) | copy-done | bytes 2097176
  3.1 0.0 copy-start.1
  3.1 1.6 %copy-done.1 = bf16[1,2048,512]{2,1,0:T(8,128)(2,1)S(1)} copy-done((bf16[1,2048,512]{2,1,0:T(8,128)(2,1)S(1)}, bf16[1,2048,512]{2,1,0:T(8,128)(2,1)}, u32[]{:S(2)}) %copy-start.1) | copy-done | bytes 2097176
  4.7 0.0 copy-start.2
  4.7 0.9 %copy-done.2 = bf16[1,64,2048]{2,1,0:T(8,128)(2,1)S(1)} copy-done((bf16[1,64,2048]{2,1,0:T(8,128)(2,1)S(1)}, bf16[1,64,2048]{2,1,0:T(8,128)(2,1)}, u32[]{:S(2)}) %copy-start.2) | copy-done | bytes 262168
  5.7 0.0 copy-start.3
  5.7 0.9 %copy-done.3 = bf16[1,64,1024]{2,1,0:T(8,128)(2,1)S(1)} copy-done((bf16[1,64,1024]{2,1,0:T(8,128)(2,1)S(1)}, bf16[1,64,1024]{2,1,0:T(8,128)(2,1)}, u32[]{:S(2)}) %copy-start.3) | copy-done | bytes 131096
  6.6 0.0 copy-start.4
  6.6 0.9 %copy-done.4 = bf16[1,64,1024]{2,1,0:T(8,128)(2,1)S(1)} copy-done((bf16[1,64,1024]{2,1,0:T(8,128)(2,1)S(1)}, bf16[1,64,1024]{2,1,0:T(8,128)(2,1)}, u32[]{:S(2)}) %copy-start.4) | copy-done | bytes 131096
  7.5 0.0 copy-start.5
  7.5 0.9 %copy-done.5 = bf16[1,64,1024]{2,1,0:T(8,128)(2,1)S(1)} copy-done((bf16[1,64,1024]{2,1,0:T(8,128)(2,1)S(1)}, bf16[1,64,1024]{2,1,0:T(8,128)(2,1)}, u32[]{:S(2)}) %copy-start.5) | copy-done | bytes 131096
  8.4 0.0 copy-start.6
  8.4 0.7 %copy-done.6 = f32[2048]{0:T(1024)S(1)} copy-done((f32[2048]{0:T(1024)S(1)}, f32[2048]{0:T(1024)}, u32[]{:S(2)}) %copy-start.6) | copy-done | bytes 8216
  9.1 46.4 %shard_map.109 = bf16[1,64,2048]{2,1,0:T(8,128)(2,1)S(1)} custom-call(bf16[1,64,1024]{2,1,0:T(8,128)(2,1)S(1)} %copy-done.3, bf16[1,64,1024]{2,1,0:T(8,128)(2,1)S(1)} %copy-done.4, bf16[1,64,1024]{2,1,0:T(8,128)(2,1)S(1)} %copy-done.5, bf16[1,64,2048]{2,1,0:T(8,128)(2,1)S(1)} %copy-done.2, bf16[1024,2048]{1,0:T(8,128)(2,1)} %wo_hbm.1, ...), custom_call_target="tpu_custom_call" | custom-call | tf_op jit(solution)/shard_map/pallas_call | solution.py:338
  55.5 0.7 %copy.15 = bf16[1,64,2048]{2,1,0:T(8,128)(2,1)} copy(bf16[1,64,2048]{2,1,0:T(8,128)(2,1)S(1)} %shard_map.109) | data formatting | bytes 524288
Async XLA Ops:
  1.5 1.6 %copy-start = (bf16[1,2048,512]{2,1,0:T(8,128)(2,1)S(1)}, bf16[1,2048,512]{2,1,0:T(8,128)(2,1)}, u32[]{:S(2)}) copy-start(bf16[1,2048,512]{2,1,0:T(8,128)(2,1)} %wg_hbm.1) | copy-start | bytes 6291460
  3.1 1.6 %copy-start.1 = (bf16[1,2048,512]{2,1,0:T(8,128)(2,1)S(1)}, bf16[1,2048,512]{2,1,0:T(8,128)(2,1)}, u32[]{:S(2)}) copy-start(bf16[1,2048,512]{2,1,0:T(8,128)(2,1)} %wu_hbm.1) | copy-start | bytes 6291460
  4.7 0.9 %copy-start.2 = (bf16[1,64,2048]{2,1,0:T(8,128)(2,1)S(1)}, bf16[1,64,2048]{2,1,0:T(8,128)(2,1)}, u32[]{:S(2)}) copy-start(bf16[1,64,2048]{2,1,0:T(8,128)(2,1)} %res_hbm.1) | copy-start | bytes 786436
  5.7 0.9 %copy-start.3 = (bf16[1,64,1024]{2,1,0:T(8,128)(2,1)S(1)}, bf16[1,64,1024]{2,1,0:T(8,128)(2,1)}, u32[]{:S(2)}) copy-start(bf16[1,64,1024]{2,1,0:T(8,128)(2,1)} %q_hbm.1) | copy-start | bytes 393220
  6.6 0.9 %copy-start.4 = (bf16[1,64,1024]{2,1,0:T(8,128)(2,1)S(1)}, bf16[1,64,1024]{2,1,0:T(8,128)(2,1)}, u32[]{:S(2)}) copy-start(bf16[1,64,1024]{2,1,0:T(8,128)(2,1)} %k_hbm.1) | copy-start | bytes 393220
  7.5 0.9 %copy-start.5 = (bf16[1,64,1024]{2,1,0:T(8,128)(2,1)S(1)}, bf16[1,64,1024]{2,1,0:T(8,128)(2,1)}, u32[]{:S(2)}) copy-start(bf16[1,64,1024]{2,1,0:T(8,128)(2,1)} %v_hbm.1) | copy-start | bytes 393220
  8.4 0.7 %copy-start.6 = (f32[2048]{0:T(1024)S(1)}, f32[2048]{0:T(1024)}, u32[]{:S(2)}) copy-start(f32[2048]{0:T(1024)} %param.16) | copy-start | bytes 24580
